TPU v7x, 32 devices: a whole 2x2x4 slice. The times are simulated.
32 devices in a mesh: pipe: 2 (over x), expert: 16 (over z, y, core).
Axes of the slice: x: 2, y: 2, z: 4, core: 2. Of those that a mesh axis runs over, the one named last changes fastest.
Arguments:
- out_grad: bfloat16 [2, 2048, 2560], P('pipe', 'expert'), may hold values from -1.5 to 1.5
- layer_input: bfloat16 [2, 2048, 2560], P('pipe', 'expert'), may hold values from -6 to 6
- route_ids: int32 [2, 2048, 6], P('pipe', 'expert'), may hold values from 0 to 15, all different within a row; in each aligned block of 128 rows (0 to 127, 128 to 255, ..., all dimensions but the last counted through in order) at most 56 rows name the same one
- route_probs: float32 [2, 2048, 6], P('pipe', 'expert'), may hold values from 0.03 to 0.5
- gate_weight: bfloat16 [2, 16, 2560, 768], P('pipe', 'expert'), may hold values from -0.125 to 0.125
- up_weight: bfloat16 [2, 16, 2560, 768], P('pipe', 'expert'), may hold values from -0.125 to 0.125
- down_weight: bfloat16 [2, 16, 768, 2560], P('pipe', 'expert'), may hold values from -0.21875 to 0.21875
Outputs:
- prev_grad: bfloat16 [2, 2048, 2560], P('pipe', 'expert')
- gate_grad: bfloat16 [2, 2048, 6], P('pipe', 'expert')
Inputs may be any that keep to these rules, and one draw needn't show every extreme that they name: `route_ids`: each token names 6 different experts; the 128 tokens of one aligned block name one expert at most 56 times, and some block reaches 56.
All inputs are finite; a program needn't handle non-finite values.
Results may differ from a plain program's by a relative error of at most 0.004.
Values may be sent and summed in bfloat16 or wider, within the bound.
A program may use at most 128 MiB of HBM per device.

v0:
```python
import jax
import jax.numpy as jnp
from jax import lax
from jax.sharding import PartitionSpec as P


def as_sent(array):
    return jax.tree.map(lambda a: a.astype(jnp.bfloat16) if a.dtype == jnp.float32 else a, array)


def partner(value, axis, distance):
    mask = 2**distance
    pairs = [(source, source ^ mask) for source in range(lax.axis_size(axis))]
    return lax.ppermute(value, axis, pairs)


def passed_along(value, axis, steps):
    count = lax.axis_size(axis)
    first, last = (max(0, -steps), min(count, count - steps))
    return lax.ppermute(value, axis, [(source, source + steps) for source in range(first, last)])


def expert_rows(pieces, gate_matrix, up_matrix, down_matrix):
    grad_rows, input_rows = pieces
    lead = grad_rows.shape[:-1]
    width = grad_rows.shape[-1]
    grad_flat = grad_rows.reshape(-1, width)
    input_flat = input_rows.reshape(-1, width)
    gate_pre = jnp.dot(input_flat, gate_matrix, preferred_element_type=jnp.float32)
    up_pre = jnp.dot(input_flat, up_matrix, preferred_element_type=jnp.float32)
    hidden_grad = jnp.dot(grad_flat, down_matrix.T, preferred_element_type=jnp.float32)
    sigmoid = jax.nn.sigmoid(gate_pre)
    active = gate_pre * sigmoid
    gate_value = jnp.sum(hidden_grad * active * up_pre, axis=-1).astype(jnp.bfloat16)
    gate_part = (hidden_grad * up_pre * sigmoid * (1.0 + gate_pre * (1.0 - sigmoid))).astype(
        jnp.bfloat16
    )
    up_part = (hidden_grad * active).astype(jnp.bfloat16)
    input_back = jnp.dot(gate_part, gate_matrix.T, preferred_element_type=jnp.float32) + jnp.dot(
        up_part, up_matrix.T, preferred_element_type=jnp.float32
    )
    return (input_back.astype(jnp.bfloat16).reshape(lead + (width,)), gate_value.reshape(lead))


def pair_rounds(pieces, trade, position, levels):
    for bit_level in range(levels):
        stride = 2**bit_level
        upper_bit = position // stride % 2
        send_half = 1 - upper_bit
        halves = [
            piece.reshape((piece.shape[0] // (2 * stride), 2, stride) + piece.shape[1:])
            for piece in pieces
        ]
        outgoing = tuple(
            (
                lax.dynamic_index_in_dim(halved, send_half, axis=1, keepdims=False)
                for halved in halves
            )
        )
        incoming = trade(outgoing, bit_level)
        pieces = tuple(
            (
                lax.dynamic_update_index_in_dim(halved, arrived, send_half, 1).reshape(piece.shape)
                for piece, halved, arrived in zip(pieces, halves, incoming)
            )
        )
    return pieces


def body(out_grad, layer_input, route_ids, route_probs, gate_weight, up_weight, down_weight):
    grad_tokens = out_grad[0]
    input_tokens = layer_input[0]
    chosen = route_ids[0]
    slot_probs = route_probs[0]
    gate_matrix = gate_weight[0, 0]
    up_matrix = up_weight[0, 0]
    down_matrix = down_weight[0, 0]
    peer_count = lax.axis_size("expert")
    token_count, top_count = chosen.shape
    model_width = grad_tokens.shape[1]
    capacity = min(token_count, 7 * token_count * top_count // (6 * peer_count))
    flat_ids = chosen.reshape(-1)
    one_hot = (flat_ids[:, None] == jnp.arange(peer_count, dtype=jnp.int32)[None, :]).astype(
        jnp.int32
    )
    places = jnp.sum(one_hot * jnp.cumsum(one_hot, axis=0), axis=1) - 1
    target = flat_ids * capacity + places
    source = (
        jnp.full((peer_count * capacity,), -1, jnp.int32)
        .at[target]
        .set(jnp.arange(token_count * top_count, dtype=jnp.int32))
    )
    filled = (source >= 0)[:, None]
    token_index = jnp.maximum(source, 0) // top_count
    zero_value = jnp.zeros((), grad_tokens.dtype)
    send_grad = jnp.where(filled, grad_tokens[token_index], zero_value).reshape(
        peer_count, capacity, model_width
    )
    send_input = jnp.where(filled, input_tokens[token_index], zero_value).reshape(
        peer_count, capacity, model_width
    )
    position = lax.axis_index("expert")
    levels = peer_count.bit_length() - 1

    def send_trade(outgoing, bit_level):
        return jax.tree.map(
            lambda part, own: part.astype(own.dtype),
            partner(as_sent(outgoing), "expert", bit_level),
            outgoing,
        )

    def return_trade(outgoing, bit_level):
        return jax.tree.map(
            lambda part, own: part.astype(own.dtype),
            partner(as_sent(outgoing), "expert", bit_level),
            outgoing,
        )

    arrived = pair_rounds((send_grad, send_input), send_trade, position, levels)
    returned, gate_back = pair_rounds(
        expert_rows(arrived, gate_matrix, up_matrix, down_matrix), return_trade, position, levels
    )
    returned_flat = returned.reshape(peer_count * capacity, model_width)
    combined = grad_tokens.astype(jnp.float32)
    target_table = target.reshape(token_count, top_count)
    for choice_index in range(top_count):
        rows_back = returned_flat[target_table[:, choice_index]]
        combined = combined + slot_probs[:, choice_index][:, None] * rows_back.astype(jnp.float32)
    gate_slot = gate_back.reshape(-1)[target].reshape(token_count, top_count)
    passed = passed_along(combined.astype(jnp.bfloat16), "pipe", -1)
    return (passed[None], gate_slot[None])


def solution(mesh):
    placed = (
        P("pipe", "expert", None),
        P("pipe", "expert", None),
        P("pipe", "expert", None),
        P("pipe", "expert", None),
        P("pipe", "expert", None, None),
        P("pipe", "expert", None, None),
        P("pipe", "expert", None, None),
    )
    return jax.shard_map(
        body,
        mesh=mesh,
        in_specs=placed,
        out_specs=(P("pipe", "expert", None), P("pipe", "expert", None)),
        check_vma=False,
    )
```

profile of v0, /device:TPU:24, one launch (start us, length us, event | category | flops | bytes accessed | tf_op | source)
XLA Modules:
  0.0 655.4 jit_solution(12016825412698760021)
XLA Ops:
  0.7 0.9 copy.16
  1.8 1.7 reduce-window.6
  4.1 3.4 scatter_custom_fusion
  7.7 5.3 gather_fusion.1
  13.0 5.3 gather_fusion
  18.3 5.7 broadcast_select_fusion.1
  24.0 4.8 dynamic-slice_bitcast_fusion.11
  28.8 1.5 dynamic-slice_bitcast_fusion.7
  30.3 0.5 collective-permute-start.4
  30.9 2.7 collective-permute-done
  33.6 3.2 bitcast_dynamic-update-slice_fusion.11
  36.8 3.3 dynamic-slice_bitcast_fusion.10
  40.1 1.5 collective-permute-start.1
  41.7 1.9 bitcast_dynamic-update-slice_fusion.7
  43.6 2.1 copy-done.6
  45.6 1.6 dynamic-slice_bitcast_fusion.6
  47.2 0.5 collective-permute-start.5
  47.7 45.4 %collective-permute-done.1 = bf16[4,2,56,2560]{3,2,1,0:T(8,128)(2,1)} collective-permute-done((bf16[4,2,56,2560]{3,2,1,0:T(8,128)(2,1)}, bf16[4,2,56,2560]{3,2,1,0:T(8,128)(2,1)}, u32[]{:S(2)}, u32[]{:S(2)}) %collective-permute-start.1) | collective-permute-done | bytes 2293792 | tf_op jit(solution)/shard_map/ppermute | solution.py:14
  93.1 3.2 bitcast_dynamic-update-slice_fusion.10
  96.3 3.3 dynamic-slice_bitcast_fusion.9
  99.7 0.5 collective-permute-start.2
  100.1 41.3 %collective-permute-done.5 = bf16[4,2,56,2560]{3,2,1,0:T(8,128)(2,1)} collective-permute-done((bf16[4,2,56,2560]{3,2,1,0:T(8,128)(2,1)}, bf16[4,2,56,2560]{3,2,1,0:T(8,128)(2,1)}, u32[]{:S(2)}, u32[]{:S(2)}) %collective-permute-start.5) | collective-permute-done | bytes 2293792 | tf_op jit(solution)/shard_map/ppermute | solution.py:14
  141.4 1.9 bitcast_dynamic-update-slice_fusion.6
  143.3 2.1 copy-done.8
  145.4 1.5 dynamic-slice_bitcast_fusion.5
  147.0 0.5 collective-permute-start.6
  147.4 3.6 collective-permute-done.2
  151.0 3.2 bitcast_dynamic-update-slice_fusion.9
  154.2 1.9 dynamic-slice_bitcast_fusion.8
  156.1 0.4 collective-permute-start.3
  156.5 85.5 %collective-permute-done.6 = bf16[2,4,56,2560]{3,2,1,0:T(8,128)(2,1)} collective-permute-done((bf16[2,4,56,2560]{3,2,1,0:T(8,128)(2,1)}, bf16[2,4,56,2560]{3,2,1,0:T(8,128)(2,1)}, u32[]{:S(2)}, u32[]{:S(2)}) %collective-permute-start.6) | collective-permute-done | bytes 2293792 | tf_op jit(solution)/shard_map/ppermute | solution.py:14
  242.0 1.9 bitcast_dynamic-update-slice_fusion.5
  244.2 64.0 %collective-permute-done.3 = bf16[1,8,56,2560]{3,2,1,0:T(8,128)(2,1)S(1)} collective-permute-done((bf16[1,8,56,2560]{3,2,1,0:T(8,128)(2,1)S(1)}, bf16[1,8,56,2560]{3,2,1,0:T(8,128)(2,1)S(1)}, u32[]{:S(2)}, u32[]{:S(2)}) %collective-permute-start.3) | collective-permute-done | bytes 2293792 | tf_op jit(solution)/shard_map/ppermute | solution.py:14
  308.4 4.2 fusion.7
  312.7 40.2 %collective-permute-done.7 = bf16[1,8,56,2560]{3,2,1,0:T(8,128)(2,1)S(1)} collective-permute-done((bf16[1,8,56,2560]{3,2,1,0:T(8,128)(2,1)S(1)}, bf16[1,8,56,2560]{3,2,1,0:T(8,128)(2,1)S(1)}, u32[]{:S(2)}, u32[]{:S(2)}) %collective-permute-start.7) | collective-permute-done | bytes 2293792 | tf_op jit(solution)/shard_map/ppermute | solution.py:14
  353.2 5.9 fusion.2
  359.1 7.5 %multiply_reduce_fusion = (bf16[896]{0:T(1024)(128)(2,1)S(1)}, f32[896,768]{0,1:T(8,128)}) fusion(f32[896,768]{0,1:T(8,128)S(1)} %fusion.7, f32[896,768]{0,1:T(8,128)} %fusion.2, bf16[896,2560]{1,0:T(8,128)(2,1)S(1)} %bitcast.163, bf16[1,1,2560,768]{3,2,1,0:T(8,128)(2,1)S(1)} %copy-done.13), kind=kOutput, calls=%fused_computation.22 | convolution fusion | flops 3528031232 | bytes 16779008 | tf_op jit(solution)/shard_map/dot_general | solution.py:30
  366.6 10.5 %fusion = f32[896,2560]{1,0:T(8,128)} fusion(bf16[1,1,2560,768]{3,2,1,0:T(8,128)(2,1)S(1)} %copy-done.12, f32[896,768]{0,1:T(8,128)} %fusion.2, f32[896,768]{0,1:T(8,128)S(1)} %fusion.7, f32[896,768]{0,1:T(8,128)} %get-tuple-element.21), kind=kOutput, calls=%fused_computation.13 | convolution fusion | flops 3530096640 | bytes 21364736 | tf_op jit(solution)/shard_map/dot_general | solution.py:39
  377.2 9.0 %add_convert_fusion = bf16[896,2560]{1,0:T(8,128)(2,1)S(1)} fusion(f32[896,2560]{1,0:T(8,128)} %fusion, bf16[1,1,2560,768]{3,2,1,0:T(8,128)(2,1)S(1)} %copy-done.13, f32[896,768]{0,1:T(8,128)} %copy-done.14, f32[896,768]{0,1:T(8,128)} %fusion.2), kind=kOutput, calls=%fused_computation.10 | convolution fusion | flops 3531931648 | bytes 23199744 | tf_op jit(solution)/shard_map/dot_general | solution.py:39
  386.4 4.4 collective-permute-done.8
  391.3 1.6 collective-permute-start.9
  392.9 50.3 %collective-permute-done.9 = bf16[4,2,56,2560]{3,2,1,0:T(8,128)(2,1)S(1)} collective-permute-done((bf16[4,2,56,2560]{3,2,1,0:T(8,128)(2,1)S(1)}, bf16[4,2,56,2560]{3,2,1,0:T(8,128)(2,1)S(1)}, u32[]{:S(2)}, u32[]{:S(2)}) %collective-permute-start.9) | collective-permute-done | bytes 2293792 | tf_op jit(solution)/shard_map/ppermute | solution.py:14
  443.7 51.0 %collective-permute-done.10 = bf16[2,4,56,2560]{3,2,1,0:T(8,128)(2,1)S(1)} collective-permute-done((bf16[2,4,56,2560]{3,2,1,0:T(8,128)(2,1)S(1)}, bf16[2,4,56,2560]{3,2,1,0:T(8,128)(2,1)S(1)}, u32[]{:S(2)}, u32[]{:S(2)}) %collective-permute-start.10) | collective-permute-done | bytes 2293792 | tf_op jit(solution)/shard_map/ppermute | solution.py:14
  495.1 2.1 copy-done.3
  497.1 1.6 dynamic-slice_bitcast_fusion
  499.5 1.1 collective-permute-done.13
  500.7 1.6 collective-permute-start.14
  502.3 2.0 collective-permute-done.14
  504.7 1.5 collective-permute-start.15
  506.2 93.0 %collective-permute-done.11 = bf16[1,8,56,2560]{3,2,1,0:T(8,128)(2,1)} collective-permute-done((bf16[1,8,56,2560]{3,2,1,0:T(8,128)(2,1)}, bf16[1,8,56,2560]{3,2,1,0:T(8,128)(2,1)}, u32[]{:S(2)}, u32[]{:S(2)}) %collective-permute-start.11) | collective-permute-done | bytes 2293792 | tf_op jit(solution)/shard_map/ppermute | solution.py:14
  599.2 3.2 bitcast_dynamic-update-slice_fusion
  602.4 4.5 gather_fusion.7
  607.0 4.5 gather_fusion.6
  611.5 4.5 gather_fusion.5
  616.0 5.4 gather_fusion.4
  621.4 5.4 gather_fusion.3
  626.7 5.4 gather_fusion.2
  632.1 3.3 add_convert_fusion.1
  635.4 1.3 collective-permute-start.12
  636.9 4.5 collective-permute-done.16
  641.4 5.0 gather_fusion.8
  646.6 0.7 copy.25
  647.3 6.9 %collective-permute-done.12 = bf16[128,2560]{1,0:T(8,128)(2,1)S(1)} collective-permute-done((bf16[128,2560]{1,0:T(8,128)(2,1)}, bf16[128,2560]{1,0:T(8,128)(2,1)S(1)}, u32[]{:S(2)}, u32[]{:S(2)}) %collective-permute-start.12) | collective-permute-done | bytes 655392 | tf_op jit(solution)/shard_map/ppermute | solution.py:20
  654.2 0.8 copy.53
  (91 shorter events, 4.5 us)
Async XLA Ops:
  0.6 7.0 %copy-start = (bf16[1,128,2560]{2,1,0:T(8,128)(2,1)S(1)}, bf16[1,128,2560]{2,1,0:T(8,128)(2,1)}, u32[]{:S(2)}) copy-start(bf16[1,128,2560]{2,1,0:T(8,128)(2,1)} %param.8) | copy-start | bytes 1966084
  7.7 5.4 copy-start.2
  23.9 4.9 copy-start.4
  28.8 4.8 collective-permute-start
  30.3 11.3 %collective-permute-start.4 = (bf16[8,1,56,2560]{3,2,0,1:T(8,128)(2,1)}, bf16[8,1,56,2560]{3,2,0,1:T(8,128)(2,1)}, u32[]{:S(2)}, u32[]{:S(2)}) collective-permute-start(bf16[8,1,56,2560]{3,2,0,1:T(8,128)(2,1)} %dynamic-slice_bitcast_fusion.7), channel_id=1, source_target_pairs={{0,1},{1,0},{2,3},{3,2},{4,5},{5,4},{6,7},{7,6},{8,9},{9,8},{10,11... | collective-permute-start | bytes 6881288 | tf_op jit(solution)/shard_map/ppermute | solution.py:14
  36.8 4.9 copy-start.5
  40.1 53.0 %collective-permute-start.1 = (bf16[4,2,56,2560]{3,2,1,0:T(8,128)(2,1)}, bf16[4,2,56,2560]{3,2,1,0:T(8,128)(2,1)}, u32[]{:S(2)}, u32[]{:S(2)}) collective-permute-start(bf16[4,2,56,2560]{3,2,1,0:T(8,128)(2,1)} %dynamic-slice_bitcast_fusion.10), channel_id=1, source_target_pairs={{0,2},{1,3},{2,0},{3,1},{4,6},{5,7},{6,4},{7,5},{8,10},{9,11},{10,... | collective-permute-start | bytes 6881288 | tf_op jit(solution)/shard_map/ppermute | solution.py:14
  43.6 2.1 copy-start.6
  47.2 94.2 %collective-permute-start.5 = (bf16[4,2,56,2560]{3,2,1,0:T(8,128)(2,1)}, bf16[4,2,56,2560]{3,2,1,0:T(8,128)(2,1)}, u32[]{:S(2)}, u32[]{:S(2)}) collective-permute-start(bf16[4,2,56,2560]{3,2,1,0:T(8,128)(2,1)} %dynamic-slice_bitcast_fusion.6), channel_id=1, source_target_pairs={{0,2},{1,3},{2,0},{3,1},{4,6},{5,7},{6,4},{7,5},{8,10},{9,11},{10,... | collective-permute-start | bytes 6881288 | tf_op jit(solution)/shard_map/ppermute | solution.py:14
  96.3 45.1 %copy-start.7 = (bf16[8,2,1,56,2560]{4,3,1,0,2:T(8,128)(2,1)S(1)}, bf16[8,2,1,56,2560]{4,3,1,0,2:T(8,128)(2,1)}, u32[]{:S(2)}) copy-start(bf16[8,2,1,56,2560]{4,3,1,0,2:T(8,128)(2,1)} %copy-done.6) | copy-start | bytes 13762564
  99.7 51.3 %collective-permute-start.2 = (bf16[2,4,56,2560]{3,2,1,0:T(8,128)(2,1)}, bf16[2,4,56,2560]{3,2,1,0:T(8,128)(2,1)}, u32[]{:S(2)}, u32[]{:S(2)}) collective-permute-start(bf16[2,4,56,2560]{3,2,1,0:T(8,128)(2,1)} %dynamic-slice_bitcast_fusion.9), channel_id=1, source_target_pairs={{0,4},{1,5},{2,6},{3,7},{4,0},{5,1},{6,2},{7,3},{8,12},{9,13},{10,... | collective-permute-start | bytes 6881288 | tf_op jit(solution)/shard_map/ppermute | solution.py:14
  143.3 2.1 copy-start.8
  147.0 95.0 %collective-permute-start.6 = (bf16[2,4,56,2560]{3,2,1,0:T(8,128)(2,1)}, bf16[2,4,56,2560]{3,2,1,0:T(8,128)(2,1)}, u32[]{:S(2)}, u32[]{:S(2)}) collective-permute-start(bf16[2,4,56,2560]{3,2,1,0:T(8,128)(2,1)} %dynamic-slice_bitcast_fusion.5), channel_id=1, source_target_pairs={{0,4},{1,5},{2,6},{3,7},{4,0},{5,1},{6,2},{7,3},{8,12},{9,13},{10,... | collective-permute-start | bytes 6881288 | tf_op jit(solution)/shard_map/ppermute | solution.py:14
  154.2 87.9 %copy-start.9 = (bf16[4,2,2,56,2560]{4,3,2,1,0:T(8,128)(2,1)S(1)}, bf16[4,2,2,56,2560]{4,3,2,1,0:T(8,128)(2,1)}, u32[]{:S(2)}) copy-start(bf16[4,2,2,56,2560]{4,3,2,1,0:T(8,128)(2,1)} %copy-done.8) | copy-start | bytes 13762564
  154.2 154.0 %slice-start = ((s8[4587520]{0:T(1024)(128)(4,1)}), s8[4194304]{0:T(1024)(128)(4,1)S(1)}, s32[]{:S(2)}) async-start(s8[4587520]{0:T(1024)(128)(4,1)} %bitcast.169), calls=%async_computation | async-start | bytes 8388608
  156.1 152.1 %slice-start.1 = ((s8[4587520]{0:T(1024)(128)(4,1)}), s8[393216]{0:T(1024)(128)(4,1)S(1)}, s32[]{:S(2)}) async-start(s8[4587520]{0:T(1024)(128)(4,1)} %bitcast.169), calls=%async_computation.1 | async-start | bytes 786432
  156.1 152.1 %collective-permute-start.3 = (bf16[1,8,56,2560]{3,2,1,0:T(8,128)(2,1)S(1)}, bf16[1,8,56,2560]{3,2,1,0:T(8,128)(2,1)S(1)}, u32[]{:S(2)}, u32[]{:S(2)}) collective-permute-start(bf16[1,8,56,2560]{3,2,1,0:T(8,128)(2,1)S(1)} %dynamic-slice_bitcast_fusion.8), channel_id=1, source_target_pairs={{0,8},{1,9},{2,10},{3,11},{4,12},{5,13},{6,14},{7,15},{8,0},{9,1},... | collective-permute-start | bytes 6881288 | tf_op jit(solution)/shard_map/ppermute | solution.py:14
  244.1 64.4 %copy-start.11 = (bf16[1,1,768,2560]{3,2,1,0:T(8,128)(2,1)S(1)}, bf16[1,1,768,2560]{3,2,1,0:T(8,128)(2,1)}, u32[]{:S(2)}) copy-start(bf16[1,1,768,2560]{3,2,1,0:T(8,128)(2,1)} %param.13) | copy-start | bytes 11796484
  244.1 108.8 %collective-permute-start.7 = (bf16[1,8,56,2560]{3,2,1,0:T(8,128)(2,1)S(1)}, bf16[1,8,56,2560]{3,2,1,0:T(8,128)(2,1)S(1)}, u32[]{:S(2)}, u32[]{:S(2)}) collective-permute-start(bf16[1,8,56,2560]{3,2,1,0:T(8,128)(2,1)S(1)} %dynamic-slice_bitcast_fusion.4), channel_id=1, source_target_pairs={{0,8},{1,9},{2,10},{3,11},{4,12},{5,13},{6,14},{7,15},{8,0},{9,1},... | collective-permute-start | bytes 6881288 | tf_op jit(solution)/shard_map/ppermute | solution.py:14
  312.7 53.9 %copy-start.14 = (f32[896,768]{0,1:T(8,128)}, f32[896,768]{0,1:T(8,128)S(1)}, u32[]{:S(2)}) copy-start(f32[896,768]{0,1:T(8,128)S(1)} %fusion.7) | copy-start | bytes 8257540
  312.7 40.4 %copy-start.12 = (bf16[1,1,2560,768]{3,2,1,0:T(8,128)(2,1)S(1)}, bf16[1,1,2560,768]{3,2,1,0:T(8,128)(2,1)}, u32[]{:S(2)}) copy-start(bf16[1,1,2560,768]{3,2,1,0:T(8,128)(2,1)} %param.11) | copy-start | bytes 11796484
  353.1 6.0 copy-start.13
  386.3 4.5 collective-permute-start.8
  391.3 52.0 %collective-permute-start.9 = (bf16[4,2,56,2560]{3,2,1,0:T(8,128)(2,1)S(1)}, bf16[4,2,56,2560]{3,2,1,0:T(8,128)(2,1)S(1)}, u32[]{:S(2)}, u32[]{:S(2)}) collective-permute-start(bf16[4,2,56,2560]{3,2,1,0:T(8,128)(2,1)S(1)} %dynamic-slice_bitcast_fusion.2), channel_id=1, source_target_pairs={{0,2},{1,3},{2,0},{3,1},{4,6},{5,7},{6,4},{7,5},{8,10},{9,11},{10,... | collective-permute-start | bytes 6881288 | tf_op jit(solution)/shard_map/ppermute | solution.py:14
  443.7 51.1 %collective-permute-start.10 = (bf16[2,4,56,2560]{3,2,1,0:T(8,128)(2,1)S(1)}, bf16[2,4,56,2560]{3,2,1,0:T(8,128)(2,1)S(1)}, u32[]{:S(2)}, u32[]{:S(2)}) collective-permute-start(bf16[2,4,56,2560]{3,2,1,0:T(8,128)(2,1)S(1)} %dynamic-slice_bitcast_fusion.1), channel_id=1, source_target_pairs={{0,4},{1,5},{2,6},{3,7},{4,0},{5,1},{6,2},{7,3},{8,12},{9,13},{10,... | collective-permute-start | bytes 6881288 | tf_op jit(solution)/shard_map/ppermute | solution.py:14
  495.1 2.1 copy-start.3
  495.1 3.8 copy-start.10
  498.7 100.5 %collective-permute-start.11 = (bf16[1,8,56,2560]{3,2,1,0:T(8,128)(2,1)}, bf16[1,8,56,2560]{3,2,1,0:T(8,128)(2,1)}, u32[]{:S(2)}, u32[]{:S(2)}) collective-permute-start(bf16[1,8,56,2560]{3,2,1,0:T(8,128)(2,1)} %dynamic-slice_bitcast_fusion), channel_id=1, source_target_pairs={{0,8},{1,9},{2,10},{3,11},{4,12},{5,13},{6,14},{7,15},{8,0},{9,1},... | collective-permute-start | bytes 6881288 | tf_op jit(solution)/shard_map/ppermute | solution.py:14
  499.4 1.2 collective-permute-start.13
  500.7 3.7 collective-permute-start.14
  504.7 132.1 %collective-permute-start.15 = (bf16[2,4,56]{2,1,0:T(4,128)(2,1)S(1)}, bf16[2,4,56]{2,1,0:T(4,128)(2,1)S(1)}, u32[]{:S(2)}, u32[]{:S(2)}) collective-permute-start(bf16[2,4,56]{2,1,0:T(4,128)(2,1)S(1)} %fusion.22), channel_id=1, source_target_pairs={{0,4},{1,5},{2,6},{3,7},{4,0},{5,1},{6,2},{7,3},{8,12},{9,13},{10,... | collective-permute-start | bytes 2696 | tf_op jit(solution)/shard_map/ppermute | solution.py:14
  632.1 22.9 %copy-start.1 = (bf16[1,128,2560]{2,1,0:T(8,128)(2,1)S(1)}, bf16[1,128,2560]{2,1,0:T(8,128)(2,1)}, u32[]{:S(2)}) copy-start(bf16[1,128,2560]{2,1,0:T(8,128)(2,1)} %param.8) | copy-start | bytes 1966084
  635.4 18.7 %collective-permute-start.12 = (bf16[128,2560]{1,0:T(8,128)(2,1)}, bf16[128,2560]{1,0:T(8,128)(2,1)S(1)}, u32[]{:S(2)}, u32[]{:S(2)}) collective-permute-start(bf16[128,2560]{1,0:T(8,128)(2,1)} %add_convert_fusion.1), channel_id=1, source_target_pairs={{16,0},{17,1},{18,2},{19,3},{20,4},{21,5},{22,6},{23,7},{24,8},{25... | collective-permute-start | bytes 1966088 | tf_op jit(solution)/shard_map/ppermute | solution.py:20
  636.8 4.5 collective-permute-start.16
where the time goes:
time: 662 us; the launch traced here: 655 us
  waiting for transfers between devices  496 us (75%)
  local copies, waits for them, and re-layouts  99 us (15%)
  matrix products  37.2 us (6%)
  other arithmetic  11.2 us (2%)
  starting transfers between devices  10.2 us (2%)
    ppermute x16, waiting for transfers between devices, partner(): return lax.ppermute(value, axis, pairs)  489 us
    gather x6, local copies, waits for them, and re-layouts, body(): rows_back = returned_flat[target_table[:, choice_index]]  29.7 us
    squeeze x14, local copies, waits for them, and re-layouts, pair_rounds(): lax.dynamic_index_in_dim(halved, send_half, axis=1, keepdims=False)  20.4 us
    dynamic_update_slice x18, local copies, waits for them, and re-layouts, pair_rounds(): lax.dynamic_update_index_in_dim(halved, arrived, send_half, 1)  20.1 us
  transfers between devices with their start and end apart: 17, of which 15 were waited for; matrix products, arithmetic and copies ran while one was open for 12% of the time, Pallas kernels for 0%

commit v1 on v0

v1 whole, which is shorter than its diff:
```python
import jax
import jax.numpy as jnp
from jax import lax
from jax.sharding import PartitionSpec as P

F32, BF16 = jnp.float32, jnp.bfloat16


def body(out_grad, layer_input, route_ids, route_probs, gate_weight, up_weight, down_weight):
    grad, inputs, ids, probs = out_grad[0], layer_input[0], route_ids[0], route_probs[0]
    gate_w, up_w, down_w = gate_weight[0, 0], up_weight[0, 0], down_weight[0, 0]
    peers = lax.axis_size("expert")
    tokens, top = ids.shape
    cap = min(tokens, 7 * tokens * top // (6 * peers))
    chosen = ids[:, :, None] == jnp.arange(peers, dtype=jnp.int32)
    weights = jnp.sum(jnp.where(chosen, probs[:, :, None], 0.0), axis=1).T
    mine = lax.all_to_all(weights, "expert", 0, 0, tiled=True)
    grad_all = lax.all_gather(grad, "expert")
    input_all = lax.all_gather(inputs, "expert")
    used = mine > 0
    place = jnp.cumsum(used.astype(jnp.int32), axis=1) - 1
    pick = (place[:, None, :] == jnp.arange(cap)[None, :, None]) & used[:, None, :]
    pick16 = pick.astype(BF16)
    grad_rows = jnp.einsum("bst,btd->bsd", pick16, grad_all).reshape(peers * cap, -1)
    input_rows = jnp.einsum("bst,btd->bsd", pick16, input_all).reshape(peers * cap, -1)
    gate_pre = jnp.dot(input_rows, gate_w, preferred_element_type=F32)
    up_pre = jnp.dot(input_rows, up_w, preferred_element_type=F32)
    hidden = lax.dot_general(grad_rows, down_w, (((1,), (1,)), ((), ())), preferred_element_type=F32)
    sig = jax.nn.sigmoid(gate_pre)
    active = gate_pre * sig
    gate_value = jnp.sum(hidden * active * up_pre, axis=-1).reshape(peers, cap)
    gate_part = (hidden * up_pre * sig * (1.0 + gate_pre * (1.0 - sig))).astype(BF16)
    up_part = (hidden * active).astype(BF16)
    back = jnp.dot(gate_part, gate_w.T, preferred_element_type=F32) + jnp.dot(
        up_part, up_w.T, preferred_element_type=F32
    )
    slot_weight = jnp.sum(jnp.where(pick, mine[:, None, :], 0.0), axis=2)
    back = (back.astype(BF16).astype(F32) * slot_weight.reshape(-1, 1)).astype(BF16)
    part = jnp.einsum("bst,bsd->btd", pick16, back.reshape(peers, cap, -1))
    total = lax.psum_scatter(part, "expert", scatter_dimension=0, tiled=False)
    combined = grad.astype(F32) + total.astype(F32)
    gates = jnp.sum(jnp.where(pick, gate_value[:, :, None], 0.0), axis=1)
    gates = lax.all_to_all(gates, "expert", 0, 0, tiled=True)
    gate_slot = jnp.sum(jnp.where(chosen, gates.T[:, None, :], 0.0), axis=2).astype(BF16)
    count = lax.axis_size("pipe")
    passed = lax.ppermute(combined.astype(BF16), "pipe", [(s, s - 1) for s in range(1, count)])
    return passed[None], gate_slot[None]


def solution(mesh):
    rows = P("pipe", "expert", None)
    mats = P("pipe", "expert", None, None)
    return jax.shard_map(
        body,
        mesh=mesh,
        in_specs=(rows,) * 4 + (mats,) * 3,
        out_specs=(rows, rows),
        check_vma=False,
    )
```

time: 662 us -> 374 us (0.56)
  waiting for transfers between devices: 496 us -> 281 us
  local copies, waits for them, and re-layouts: 99 us -> 4.58 us
  blocking collectives: 0 us -> 18.2 us
  between operations: 1.68 us -> 13.9 us
  matrix products: 37.2 us -> 49.1 us
  starting transfers between devices: 10.2 us -> 1.41 us
  other arithmetic: 11.2 us -> 2.51 us
    ppermute x17 -> x1, waiting for transfers between devices: 496 us -> 7.39 us  [body(): lax.ppermute(combined.astype(BF16), 'pipe', [(s, s - 1) for s in range(1,...]
    all_gather x0 -> x2, waiting for transfers between devices: none -> 154 us  [the longest x1 77.8 us: body(): input_all = lax.all_gather(inputs, 'expert')]
    reduce_scatter x0 -> x1, waiting for transfers between devices: none -> 118 us  [body(): total = lax.psum_scatter(part, 'expert', scatter_dimension=0, tiled=False)]
    gather x9 -> x0, local copies, waits for them, and re-layouts: 45.3 us -> none  [the longest x6 29.7 us: body(): rows_back = returned_flat[target_table[:, choice_index]]]
    squeeze x14 -> x0, local copies, waits for them, and re-layouts: 20.4 us -> none  [pair_rounds(): lax.dynamic_index_in_dim(halved, send_half, axis=1, keepdims=False)]
    dynamic_update_slice x18 -> x0, local copies, waits for them, and re-layouts: 20.1 us -> none  [pair_rounds(): lax.dynamic_update_index_in_dim(halved, arrived, send_half, 1)]
    all_to_all x0 -> x2, blocking collectives: none -> 18.2 us  [the longest x1 9.1 us: body(): mine = lax.all_to_all(weights, 'expert', 0, 0, tiled=True)]
    dot_general x5 -> x8, matrix products: 37.2 us -> 49.1 us  [the longest x1 10.5 us: body(): jnp.dot(up_part, up_w.T, preferred_element_type=F32)]
  transfers between devices with their start and end apart: 17 -> 4, of which waited for: 15 -> 4; matrix products, arithmetic and copies ran while one was open for 12% -> 3% of each run, Pallas kernels for 0% -> 0%
where the time goes in v1:
time: 374 us; the launch traced here: 371 us
  waiting for transfers between devices  281 us (75%)
  matrix products  49.1 us (13%)
  blocking collectives  18.2 us (5%)
  between operations  13.9 us (4%)
  local copies, waits for them, and re-layouts  4.58 us (1%)
    reduce_scatter x1, waiting for transfers between devices, body(): total = lax.psum_scatter(part, 'expert', scatter_dimension=0, tiled=False)  118 us
    all_gather x1, waiting for transfers between devices, body(): input_all = lax.all_gather(inputs, 'expert')  77.8 us
    all_gather x1, waiting for transfers between devices, body(): grad_all = lax.all_gather(grad, 'expert')  76.1 us
    dot_general x1, matrix products, body(): jnp.dot(up_part, up_w.T, preferred_element_type=F32)  10.5 us
    all_to_all x1, blocking collectives, body(): mine = lax.all_to_all(weights, 'expert', 0, 0, tiled=True)  9.1 us
    all_to_all x1, blocking collectives, body(): gates = lax.all_to_all(gates, 'expert', 0, 0, tiled=True)  9.07 us
    dot_general x1, matrix products, body(): jnp.dot(gate_part, gate_w.T, preferred_element_type=F32)  7.98 us
  transfers between devices with their start and end apart: 4, of which 4 were waited for; matrix products, arithmetic and copies ran while one was open for 3% of the time, Pallas kernels for 0%

profile of v1, /device:TPU:24, one launch (start us, length us, event | category | flops | bytes accessed | tf_op | source)
XLA Modules:
  0.0 370.5 jit_solution(7103586337763738563)
XLA Ops:
  7.2 0.0 all-gather.5.cloned.1.call-start
  7.2 0.7 all-gather.5.cloned.1.call-update
  7.9 0.0 all-gather.3.cloned.1.call-start
  7.9 0.7 all-gather.3.cloned.1.call-update
  8.6 0.0 reduce-scatter.2.cloned.1.call-start
  8.7 0.7 copy.28
  9.4 0.7 copy.27
  10.1 9.1 %all_to_all.24 = f32[16,1,128]{2,1,0:T(1,128)S(1)} all-to-all(f32[16,1,128]{2,1,0:T(1,128)S(1)} %bitcast.64), channel_id=1, replica_groups=mesh['pipe'=2,'expert'=16] {'expert'}, dimensions={0} | all-to-all | bytes 16384 | tf_op jit(solution)/shard_map/all_to_all | solution.py:17
  19.2 0.3 reduce_window_sum.17
  19.5 77.8 %all-gather.5.cloned.1.call-done = bf16[16,128,2560]{2,1,0:T(8,128)(2,1)} async-done(((bf16[1,128,2560]{2,1,0:T(8,128)(2,1)}), bf16[16,128,2560]{2,1,0:T(8,128)(2,1)}) %all-gather.5.cloned.1.call-update) | async-done | bytes 10485776 | tf_op jit(solution)/shard_map/all_gather | solution.py:19
  97.3 0.0 copy-start.3
  97.3 5.6 %fusion.15 = bf16[16,56,2560]{2,1,0:T(8,128)(2,1)S(1)} fusion(bf16[16,128,2560]{2,1,0:T(8,128)(2,1)} %all-gather.5.cloned.1.call-done, s32[16,128]{1,0:T(8,128)S(1)} %broadcast_add_fusion, pred[16,128]{1,0:T(8,128)(4,1)S(1)} %get-tuple-element.5), kind=kOutput, calls=%fused_computation.24 | convolution fusion | flops 587431936 | bytes 15083520 | tf_op jit(solution)/shard_map/bst,btd->bsd/dot_general | solution.py:25
  102.9 0.0 copy-start
  102.9 2.2 copy-done
  105.1 0.0 copy-done.3
  105.1 4.4 %fusion.2 = f32[896,768]{0,1:T(8,128)S(1)} fusion(bf16[896,2560]{1,0:T(8,128)(2,1)S(1)} %bitcast.52, bf16[1,1,2560,768]{3,2,1,0:T(8,128)(2,1)S(1)} %copy-done.3), kind=kOutput, calls=%fused_computation.4 | convolution fusion | flops 3523215360 | bytes 11272192 | tf_op jit(solution)/shard_map/dot_general | solution.py:26
  109.5 76.1 %all-gather.3.cloned.1.call-done = bf16[16,128,2560]{2,1,0:T(8,128)(2,1)} async-done(((bf16[1,128,2560]{2,1,0:T(8,128)(2,1)}), bf16[16,128,2560]{2,1,0:T(8,128)(2,1)}) %all-gather.3.cloned.1.call-update) | async-done | bytes 10485776 | tf_op jit(solution)/shard_map/all_gather | solution.py:18
  185.7 0.0 copy-start.2
  185.7 0.0 slice-start
  185.7 5.6 %fusion.17 = bf16[16,56,2560]{2,1,0:T(8,128)(2,1)S(1)} fusion(bf16[16,128,2560]{2,1,0:T(8,128)(2,1)} %all-gather.3.cloned.1.call-done, s32[16,128]{1,0:T(8,128)S(1)} %broadcast_add_fusion, pred[16,128]{1,0:T(8,128)(4,1)S(1)} %get-tuple-element.5), kind=kOutput, calls=%fused_computation.25 | convolution fusion | flops 587431936 | bytes 15083520 | tf_op jit(solution)/shard_map/bst,btd->bsd/dot_general | solution.py:24
  191.3 0.0 copy-done.2
  191.3 0.0 slice-start.1
  191.3 0.0 copy-start.5
  191.3 4.2 %fusion.7 = f32[896,768]{0,1:T(8,128)S(1)} fusion(bf16[896,2560]{1,0:T(8,128)(2,1)S(1)} %bitcast.56, bf16[1,1,768,2560]{3,2,1,0:T(8,128)(2,1)S(1)} %copy-done.2), kind=kOutput, calls=%fused_computation.9 | convolution fusion | flops 3523215360 | bytes 11272192 | tf_op jit(solution)/shard_map/dot_general | solution.py:28
  195.6 0.0 slice-done
  195.6 0.0 slice-done.1
  195.6 0.0 copy-done.5
  195.6 0.0 copy-start.6
  195.6 0.0 copy-start.4
  195.6 5.2 %multiply_reduce_fusion = (f32[896]{0:T(1024)S(1)}, f32[896,768]{0,1:T(8,128)S(1)}) fusion(f32[896,768]{0,1:T(8,128)S(1)} %fusion.7, f32[896,768]{0,1:T(8,128)S(1)} %fusion.2, bf16[896,2560]{1,0:T(8,128)(2,1)S(1)} %bitcast.55, bf16[1,1,2560,768]{3,2,1,0:T(8,128)(2,1)S(1)} %copy-done.5), kind=kOutput, calls=%fused_computation.11 | convolution fusion | flops 3528031232 | bytes 16780800 | tf_op jit(solution)/shard_map/dot_general | solution.py:27
  200.9 0.0 copy-done.6
  200.9 0.0 copy-done.4
  200.9 8.0 %fusion = f32[896,2560]{1,0:T(8,128)} fusion(bf16[1,1,2560,768]{3,2,1,0:T(8,128)(2,1)S(1)} %copy-done.4, f32[896,768]{0,1:T(8,128)S(1)} %fusion.2, f32[896,768]{0,1:T(8,128)S(1)} %fusion.7, f32[896,768]{0,1:T(8,128)S(1)} %get-tuple-element.7), kind=kOutput, calls=%fused_computation.2 | convolution fusion | flops 3530096640 | bytes 21364736 | tf_op jit(solution)/shard_map/dot_general | solution.py:34
  208.9 0.1 broadcast_in_dim.64
  208.9 0.4 select_reduce_fusion
  209.3 0.1 mul.38
  209.4 10.5 %multiply_convert_fusion = bf16[896,2560]{1,0:T(8,128)(2,1)S(1)} fusion(f32[896,2560]{1,0:T(8,128)} %fusion, f32[896]{0:T(1024)S(1)} %mul.38, bf16[1,1,2560,768]{3,2,1,0:T(8,128)(2,1)} %param.12, f32[896,768]{0,1:T(8,128)} %copy-done.6, f32[896,768]{0,1:T(8,128)S(1)} %fusion.2), kind=kOutput, calls=%fused_computation | convolution fusion | flops 3538812928 | bytes 23203328 | tf_op jit(solution)/shard_map/dot_general | solution.py:34
  219.9 5.6 %fusion.13 = bf16[16,128,2560]{2,1,0:T(8,128)(2,1)} fusion(bf16[16,56,2560]{2,1,0:T(8,128)(2,1)S(1)} %bitcast.57, s32[16,128]{1,0:T(8,128)S(1)} %broadcast_add_fusion, pred[16,128]{1,0:T(8,128)(4,1)S(1)} %get-tuple-element.5), kind=kOutput, calls=%fused_computation.23 | convolution fusion | flops 587431936 | bytes 15083520 | tf_op jit(solution)/shard_map/bst,bsd->btd/dot_general | solution.py:39
  225.4 0.0 copy-start.1
  225.4 0.0 reduce-scatter.2.cloned.1.call-update
  225.5 118.1 %reduce-scatter.2.cloned.1.call-done = bf16[1,128,2560]{2,1,0:T(8,128)(2,1)} async-done(((bf16[16,128,2560]{2,1,0:T(8,128)(2,1)}), bf16[1,128,2560]{2,1,0:T(8,128)(2,1)}) %reduce-scatter.2.cloned.1.call-update) | async-done | bytes 655376 | tf_op jit(solution)/shard_map/reduce_scatter | solution.py:40
  343.6 0.0 copy-done.1
  343.6 1.2 fusion.11
  344.8 1.3 collective-permute-start
  346.1 9.1 %all_to_all.25 = f32[16,1,128]{2,1,0:T(1,128)S(1)} all-to-all(f32[16,1,128]{2,1,0:T(1,128)S(1)} %bitcast.65), channel_id=1, replica_groups=mesh['pipe'=2,'expert'=16] {'expert'}, dimensions={0} | all-to-all | bytes 16384 | tf_op jit(solution)/shard_map/all_to_all | solution.py:43
  355.2 0.6 select_reduce_fusion.2
  355.8 7.4 %collective-permute-done = bf16[128,2560]{1,0:T(8,128)(2,1)S(1)} collective-permute-done((bf16[128,2560]{1,0:T(8,128)(2,1)S(1)}, bf16[128,2560]{1,0:T(8,128)(2,1)S(1)}, u32[]{:S(2)}, u32[]{:S(2)}) %collective-permute-start) | collective-permute-done | bytes 655392 | tf_op jit(solution)/shard_map/ppermute | solution.py:46
  363.2 0.8 copy.30
  (4 shorter events, 0.0 us)
Async XLA Ops:
  7.2 90.1 %all-gather.5.cloned.1.call-start = ((), (), s32[]{:S(2)}) async-start(), calls=%async_computation.4 | async-start | bytes 11141120 | tf_op jit(solution)/shard_map/all_gather | solution.py:19
  7.9 177.8 %all-gather.3.cloned.1.call-start = ((), (), s32[]{:S(2)}) async-start(), calls=%async_computation.3 | async-start | bytes 11141120 | tf_op jit(solution)/shard_map/all_gather | solution.py:18
  8.6 334.9 %reduce-scatter.2.cloned.1.call-start = ((), (), s32[]{:S(2)}) async-start(), calls=%async_computation.5 | async-start | bytes 11141120 | tf_op jit(solution)/shard_map/reduce_scatter | solution.py:40
  97.3 7.8 %copy-start.3 = (bf16[1,1,2560,768]{3,2,1,0:T(8,128)(2,1)S(1)}, bf16[1,1,2560,768]{3,2,1,0:T(8,128)(2,1)}, u32[]{:S(2)}) copy-start(bf16[1,1,2560,768]{3,2,1,0:T(8,128)(2,1)} %param.11) | copy-start | bytes 11796484
  102.9 2.2 copy-start
  185.7 5.7 %copy-start.2 = (bf16[1,1,768,2560]{3,2,1,0:T(8,128)(2,1)S(1)}, bf16[1,1,768,2560]{3,2,1,0:T(8,128)(2,1)}, u32[]{:S(2)}) copy-start(bf16[1,1,768,2560]{3,2,1,0:T(8,128)(2,1)} %param.13) | copy-start | bytes 11796484
  185.7 9.9 %slice-start = ((s8[4587520]{0:T(1024)(128)(4,1)}), s8[4194304]{0:T(1024)(128)(4,1)S(1)}, s32[]{:S(2)}) async-start(s8[4587520]{0:T(1024)(128)(4,1)} %bitcast.53), calls=%async_computation.6 | async-start | bytes 8388608
  191.3 4.3 %slice-start.1 = ((s8[4587520]{0:T(1024)(128)(4,1)}), s8[393216]{0:T(1024)(128)(4,1)S(1)}, s32[]{:S(2)}) async-start(s8[4587520]{0:T(1024)(128)(4,1)} %bitcast.53), calls=%async_computation.7 | async-start | bytes 786432
  191.3 4.3 %copy-start.5 = (bf16[1,1,2560,768]{3,2,1,0:T(8,128)(2,1)S(1)}, bf16[1,1,2560,768]{3,2,1,0:T(8,128)(2,1)}, u32[]{:S(2)}) copy-start(bf16[1,1,2560,768]{3,2,1,0:T(8,128)(2,1)} %param.12) | copy-start | bytes 11796484
  195.6 5.2 %copy-start.6 = (f32[896,768]{0,1:T(8,128)}, f32[896,768]{0,1:T(8,128)S(1)}, u32[]{:S(2)}) copy-start(f32[896,768]{0,1:T(8,128)S(1)} %fusion.7) | copy-start | bytes 8257540
  195.6 5.2 %copy-start.4 = (bf16[1,1,2560,768]{3,2,1,0:T(8,128)(2,1)S(1)}, bf16[1,1,2560,768]{3,2,1,0:T(8,128)(2,1)}, u32[]{:S(2)}) copy-start(bf16[1,1,2560,768]{3,2,1,0:T(8,128)(2,1)} %param.11) | copy-start | bytes 11796484
  225.4 118.1 %copy-start.1 = (bf16[1,128,2560]{2,1,0:T(8,128)(2,1)S(1)}, bf16[1,128,2560]{2,1,0:T(8,128)(2,1)}, u32[]{:S(2)}) copy-start(bf16[1,128,2560]{2,1,0:T(8,128)(2,1)} %param.7) | copy-start | bytes 1966084
  344.8 18.4 %collective-permute-start = (bf16[128,2560]{1,0:T(8,128)(2,1)S(1)}, bf16[128,2560]{1,0:T(8,128)(2,1)S(1)}, u32[]{:S(2)}, u32[]{:S(2)}) collective-permute-start(bf16[128,2560]{1,0:T(8,128)(2,1)S(1)} %fusion.11), channel_id=1, source_target_pairs={{16,0},{17,1},{18,2},{19,3},{20,4},{21,5},{22,6},{23,7},{24,8},{25... | collective-permute-start | bytes 1966088 | tf_op jit(solution)/shard_map/ppermute | solution.py:46
Sparse Core Ops, SparseCore 0:
  10.3 86.9 all-gather.4
  99.6 86.0 all-gather.2
  225.6 117.9 reduce-scatter.1

commit v2 on v1

v2 whole, which is shorter than its diff:
```python
import functools

import jax
import jax.numpy as jnp
from jax import lax
from jax.experimental import pallas as pl
from jax.experimental.pallas import tpu as pltpu
from jax.sharding import PartitionSpec as P

F32, BF16 = jnp.float32, jnp.bfloat16
MESH = pl.DeviceIdType.MESH
NT = (((1,), (1,)), ((), ()))


def dot(a, b, dims=(((1,), (0,)), ((), ()))):
    return lax.dot_general(a, b, dims, preferred_element_type=F32)


def kernel(
    nz, ny, slots, pipes,
    grad_ref, input_ref, send_w_ref, gate_hbm, up_hbm, down_hbm,
    out_ref, gates_ref, all_ref,
    gate_w, up_w, down_w, blocks, rows, parts, hidden, scaled, slot_w, route, gate_send,
    core_recv, y_send, y_recv, z_send, z_recv, total, final, zeros,
    load_sem, own_sem, block_sem, zero_sem, ag_send, ag_recv, w_send, w_recv, g_send, g_recv,
    c_send_sem, c_recv_sem, y_send_sem, y_recv_sem, z_send_sem, z_recv_sem, p_sem,
):
    peers = nz * ny * 2
    count = 2 * ny
    tokens, width = grad_ref.shape
    inner = gate_w.shape[1]
    stage = lax.axis_index("pipe")
    me = lax.axis_index("expert")
    core = lax.rem(me, 2)
    yy = lax.rem(lax.div(me, 2), ny)
    zz = lax.div(me, 2 * ny)
    sibling = me + 1 - 2 * core

    def number(z, y, c):
        return (z * ny + y) * 2 + c

    def column_of(j):
        low, high = zz, nz - 1 - zz
        near = jnp.minimum(low, high)
        half = lax.div(j + 1, 2)
        between = jnp.where(lax.rem(j, 2) == 1, zz - half, zz + half)
        far = jnp.where(low <= high, j, nz - 1 - j)
        return jnp.where(j <= 2 * near, between, far)

    def remote(src, dst, ssem, rsem, target):
        return pltpu.make_async_remote_copy(
            src_ref=src, dst_ref=dst, send_sem=ssem, recv_sem=rsem,
            device_id={"expert": target}, device_id_type=MESH,
        )

    def spread(block, kind, target):
        return remote(all_ref.at[block], all_ref.at[block], ag_send.at[block, kind], ag_recv.at[block], target)

    def arrived(block):
        spread(block, 0, sibling).wait_recv()

    def y_peer(i):
        return lax.rem(yy + i, ny)

    def plane_sends(z, act):
        block = number(z, yy, core)

        @pl.when((z <= zz) & (zz + 1 < nz))
        def _():
            act(spread(block, 1, me + 2 * ny))

        @pl.when((z >= zz) & (zz > 0))
        def _():
            act(spread(block, 2, me - 2 * ny))

        for i in range(1, ny):
            act(spread(block, 2 + i, number(zz, y_peer(i), core)))
        act(spread(block, 0, sibling))

    loads = [
        pltpu.make_async_copy(gate_hbm, gate_w, load_sem.at[0]),
        pltpu.make_async_copy(up_hbm, up_w, load_sem.at[1]),
        pltpu.make_async_copy(down_hbm, down_w, load_sem.at[2]),
    ]
    own = [
        pltpu.make_async_copy(grad_ref, all_ref.at[me, 0], own_sem.at[0]),
        pltpu.make_async_copy(input_ref, all_ref.at[me, 1], own_sem.at[1]),
    ]
    for copy in own + loads:
        copy.start()

    barrier = pltpu.get_barrier_semaphore()

    @pl.loop(1, peers)
    def _(i):
        pl.semaphore_signal(barrier, inc=1, device_id={"expert": lax.rem(me + i, peers)}, device_id_type=MESH)

    @pl.when(stage > 0)
    def _():
        pl.semaphore_signal(barrier, inc=1, device_id={"pipe": stage - 1}, device_id_type=MESH)

    @pl.when(stage < pipes - 1)
    def _():
        pl.semaphore_signal(barrier, inc=1, device_id={"pipe": stage + 1}, device_id_type=MESH)

    beside = jnp.where(stage > 0, 1, 0) + jnp.where(stage < pipes - 1, 1, 0)
    pl.semaphore_wait(barrier, peers - 1 + beside)

    def w_copy(target):
        return remote(send_w_ref.at[target], route.at[me], w_send.at[target], w_recv.at[me], target)

    def w_from(source):
        return remote(send_w_ref.at[source], route.at[source], w_send.at[source], w_recv.at[source], source)

    @pl.loop(1, peers)
    def _(i):
        w_copy(lax.rem(me + i, peers)).start()

    for copy in own:
        copy.wait()
    plane_sends(zz, lambda c: c.start())
    route[me] = send_w_ref[me]

    @pl.loop(1, peers)
    def _(i):
        w_from(lax.rem(me + i, peers)).wait_recv()

    for copy in loads:
        copy.wait()

    row_at = lax.broadcasted_iota(jnp.int32, (tokens, tokens), 0)
    col_at = lax.broadcasted_iota(jnp.int32, (tokens, tokens), 1)
    before = jnp.where(row_at < col_at, 1.0, 0.0).astype(BF16)
    slot_at = lax.broadcasted_iota(jnp.int32, (slots, tokens), 0)

    def pick_of(block):
        weight = route[block]
        used = jnp.where(weight > 0, 1.0, 0.0)
        place = dot(used.astype(BF16), before)[0:1].astype(jnp.int32)
        return (place == slot_at) & (weight[0:1] > 0), weight[0:1]

    def block_in(z, i):
        return number(z, lax.rem(i, ny), lax.div(i, ny))

    def fetch(z, i):
        return pltpu.make_async_copy(all_ref.at[block_in(z, i)], blocks.at[i], block_sem.at[i])

    def compute(z):
        @pl.loop(0, count)
        def _(i):
            fetch(z, i).start()

        @pl.loop(0, count)
        def _(i):
            fetch(z, i).wait()
            pick, weight = pick_of(block_in(z, i))
            pick16 = jnp.where(pick, 1.0, 0.0).astype(BF16)
            at = pl.ds(pl.multiple_of(i * slots, slots), slots)
            rows[0, at] = dot(pick16, blocks[i, 0]).astype(BF16)
            rows[1, at] = dot(pick16, blocks[i, 1]).astype(BF16)
            per_slot = jnp.sum(jnp.where(pick, weight, 0.0), axis=1, keepdims=True)
            slot_w[0, at] = jnp.broadcast_to(per_slot, (slots, 128))

        slot_w[1] = jnp.zeros_like(slot_w[1])
        tile = 256

        @pl.loop(0, inner // tile)
        def _(f):
            at = pl.ds(pl.multiple_of(f * tile, tile), tile)
            gate_pre = dot(rows[1], gate_w[:, at])
            up_pre = dot(rows[1], up_w[:, at])
            back = dot(rows[0], down_w[at, :], NT)
            sig = jax.nn.sigmoid(gate_pre)
            up_back = back * (gate_pre * sig)
            hidden[0, :, at] = (back * up_pre * sig * (1.0 + gate_pre * (1.0 - sig))).astype(BF16)
            hidden[1, :, at] = up_back.astype(BF16)
            value = jnp.sum(up_back * up_pre, axis=1, keepdims=True)
            slot_w[1] = slot_w[1] + jnp.broadcast_to(value, slot_w[1].shape)

        wide = 512

        @pl.loop(0, width // wide)
        def _(d):
            at = pl.ds(pl.multiple_of(d * wide, wide), wide)
            back = dot(hidden[0], gate_w[at, :], NT) + dot(hidden[1], up_w[at, :], NT)
            back = back.astype(BF16).astype(F32) * slot_w[0, :, 0:1]
            scaled[:, at] = back.astype(BF16)

        @pl.loop(0, count)
        def _(i):
            block = block_in(z, i)
            pick, weight = pick_of(block)
            turned = jnp.where(pick, 1.0, 0.0).T.astype(BF16)
            at = pl.ds(pl.multiple_of(i * slots, slots), slots)
            parts[lax.div(i, ny), lax.rem(i, ny)] = dot(turned, scaled[at]).astype(BF16)
            value = jnp.sum(jnp.where(pick, slot_w[1, at, 0:1], 0.0), axis=0, keepdims=True)
            gate_send[block] = jnp.broadcast_to(value, (8, tokens))

    step = 16

    def by_rows(act):
        @pl.loop(0, tokens // step)
        def _(r):
            act(pl.ds(pl.multiple_of(r * step, step), step))

    def core_copy(j):
        slot = lax.rem(j, 2)
        return remote(parts.at[1 - core], core_recv.at[slot], c_send_sem.at[slot], c_recv_sem.at[slot], sibling)

    def y_copy(j, i):
        return remote(
            y_send.at[j, y_peer(i)], y_recv.at[j, ny - 1 - i],
            y_send_sem.at[j, i - 1], y_recv_sem.at[j, ny - 1 - i], number(zz, y_peer(i), core),
        )

    def core_finish(j):
        core_copy(j).wait()
        slot = lax.rem(j, 2)
        for y in range(ny):

            def act(at):
                both = parts[core, y, at].astype(F32) + core_recv[slot, y, at].astype(F32)
                y_send[j, y, at] = both.astype(BF16)

            by_rows(act)
        for i in range(1, ny):
            y_copy(j, i).start()

    def z_copy(z):
        return remote(
            z_send.at[z], z_recv.at[zz], z_send_sem.at[z], z_recv_sem.at[zz], number(z, yy, core)
        )

    def z_from(z):
        return remote(z_send.at[z], z_recv.at[z], z_send_sem.at[z], z_recv_sem.at[z], number(z, yy, core))

    def y_finish(j):
        z = column_of(j)
        for i in range(1, ny):
            y_copy(j, i).wait_recv()

        def summed(at):
            value = y_send[j, yy, at].astype(F32)
            for i in range(ny - 1):
                value = value + y_recv[j, i, at].astype(F32)
            return value

        @pl.when(z == zz)
        def _():
            def act(at):
                total[at] = summed(at)

            by_rows(act)

        @pl.when(z != zz)
        def _():
            def act(at):
                z_send[z, at] = summed(at).astype(BF16)

            by_rows(act)
            z_copy(z).start()

    @pl.loop(0, nz)
    def _(j):
        far = j + 1

        @pl.when(zz - far >= 0)
        def _():
            arrived(number(zz - far, yy, core))
            plane_sends(zz - far, lambda c: c.start())

        @pl.when(zz + far < nz)
        def _():
            arrived(number(zz + far, yy, core))
            plane_sends(zz + far, lambda c: c.start())

        z = column_of(j)
        for i in range(1, ny):
            block = number(z, y_peer(i), core)
            arrived(block)
            spread(block, 0, sibling).start()
        for y in range(ny):
            arrived(number(z, y, 1 - core))
        compute(z)
        core_copy(j).start()

        @pl.when(j > 0)
        def _():
            y_finish(j - 1)

        core_finish(j)

    def g_copy(target):
        return remote(gate_send.at[target], gates_ref.at[me], g_send.at[target], g_recv.at[me], target)

    def g_from(source):
        return remote(gate_send.at[source], gates_ref.at[source], g_send.at[source], g_recv.at[source], source)

    @pl.loop(1, peers)
    def _(i):
        g_copy(lax.rem(me + i, peers)).start()

    gates_ref[me] = gate_send[me]
    own_grad = pltpu.make_async_copy(grad_ref, blocks.at[0, 0], own_sem.at[0])
    own_grad.start()

    @pl.when(stage == pipes - 1)
    def _():
        zeros[...] = jnp.zeros_like(zeros)
        pltpu.make_async_copy(zeros, out_ref, zero_sem).start()

    y_finish(nz - 1)
    own_grad.wait()

    @pl.loop(0, nz)
    def _(z):
        @pl.when(z != zz)
        def _():
            z_from(z).wait_recv()

    z_recv[zz] = jnp.zeros_like(z_recv[0])

    def finish(at):
        value = blocks[0, 0, at].astype(F32) + total[at]
        for z in range(nz):
            value = value + z_recv[z, at].astype(F32)
        final[at] = value.astype(BF16)

    by_rows(finish)

    passing = pltpu.make_async_remote_copy(
        src_ref=final, dst_ref=out_ref, send_sem=p_sem.at[0], recv_sem=p_sem.at[1],
        device_id={"pipe": lax.rem(stage + pipes - 1, pipes)}, device_id_type=MESH,
    )

    @pl.when(stage > 0)
    def _():
        passing.start()

    @pl.loop(1, peers)
    def _(i):
        other = lax.rem(me + i, peers)
        g_from(other).wait_recv()
        g_copy(other).wait_send()
        w_copy(other).wait_send()

    @pl.loop(0, nz)
    def _(z):
        plane_sends(z, lambda c: c.wait_send())
        for i in range(1, ny):
            spread(number(z, y_peer(i), core), 0, sibling).wait_send()
            y_copy(z, i).wait_send()

        @pl.when(z != zz)
        def _():
            z_copy(z).wait_send()

    @pl.when(stage > 0)
    def _():
        passing.wait_send()

    @pl.when(stage < pipes - 1)
    def _():
        passing.wait_recv()

    @pl.when(stage == pipes - 1)
    def _():
        pltpu.make_async_copy(zeros, out_ref, zero_sem).wait()


def body(pipes, out_grad, layer_input, route_ids, route_probs, gate_weight, up_weight, down_weight):
    ids, probs = route_ids[0], route_probs[0]
    peers = lax.axis_size("expert")
    tokens, top = ids.shape
    width, inner = gate_weight.shape[2:]
    cap = min(tokens, 7 * tokens * top // (6 * peers))
    slots = -(-cap // 16) * 16
    chips = peers // 2
    nz = 4 if chips % 4 == 0 else chips
    ny = chips // nz
    count = 2 * ny
    chosen = ids.T[:, None, :] == jnp.arange(peers, dtype=jnp.int32)[None, :, None]
    weights = jnp.sum(jnp.where(chosen, probs.T[:, None, :], 0.0), axis=0)
    weights = jnp.broadcast_to(weights[:, None, :], (peers, 8, tokens))
    anywhere = pl.BlockSpec(memory_space=pl.ANY)
    vmem = pl.BlockSpec(memory_space=pltpu.VMEM)
    dma = pltpu.SemaphoreType.DMA
    half = (tokens, width)
    passed, gates, unused = pl.pallas_call(
        functools.partial(kernel, nz, ny, slots, pipes),
        out_shape=(
            jax.ShapeDtypeStruct(half, BF16),
            jax.ShapeDtypeStruct((peers, 8, tokens), F32),
            jax.ShapeDtypeStruct((peers, 2) + half, BF16),
        ),
        in_specs=[anywhere, anywhere, vmem, anywhere, anywhere, anywhere],
        out_specs=(anywhere, vmem, anywhere),
        scratch_shapes=[
            pltpu.VMEM((width, inner), BF16),
            pltpu.VMEM((width, inner), BF16),
            pltpu.VMEM((inner, width), BF16),
            pltpu.VMEM((count, 2) + half, BF16),
            pltpu.VMEM((2, count * slots, width), BF16),
            pltpu.VMEM((2, ny) + half, BF16),
            pltpu.VMEM((2, count * slots, inner), BF16),
            pltpu.VMEM((count * slots, width), BF16),
            pltpu.VMEM((2, count * slots, 128), F32),
            pltpu.VMEM((peers, 8, tokens), F32),
            pltpu.VMEM((peers, 8, tokens), F32),
            pltpu.VMEM((2, ny) + half, BF16),
            pltpu.VMEM((nz, ny) + half, BF16),
            pltpu.VMEM((nz, ny - 1) + half, BF16),
            pltpu.VMEM((nz,) + half, BF16),
            pltpu.VMEM((nz,) + half, BF16),
            pltpu.VMEM(half, F32),
            pltpu.VMEM(half, BF16),
            pltpu.VMEM(half, BF16),
            dma((3,)), dma((2,)), dma((count,)), dma(()),
            dma((peers, 2 + ny)), dma((peers,)), dma((peers,)), dma((peers,)),
            dma((peers,)), dma((peers,)),
            dma((2,)), dma((2,)), dma((nz, ny - 1)), dma((nz, ny - 1)), dma((nz,)), dma((nz,)), dma((2,)),
        ],
        compiler_params=pltpu.CompilerParams(
            collective_id=0, has_side_effects=True, vmem_limit_bytes=63 * 2**20
        ),
        cost_estimate=pl.CostEstimate(
            flops=10 * peers * cap * width * inner, bytes_accessed=80 * 2**20, transcendentals=0
        ),
    )(out_grad[0], layer_input[0], weights, gate_weight[0, 0], up_weight[0, 0], down_weight[0, 0])
    slot = jnp.sum(jnp.where(chosen, gates[:, 0, :][None], 0.0), axis=1)
    return passed[None], slot.T.astype(BF16)[None]


def solution(mesh):
    rows = P("pipe", "expert", None)
    mats = P("pipe", "expert", None, None)
    return jax.shard_map(
        functools.partial(body, mesh.shape["pipe"]),
        mesh=mesh,
        in_specs=(rows,) * 4 + (mats,) * 3,
        out_specs=(rows, rows),
        check_vma=False,
    )
```

time: 374 us -> 285 us (0.76)
  waiting for transfers between devices: 281 us -> 0 us
  Pallas kernels: 0 us -> 279 us
  matrix products: 49.1 us -> 0 us
  blocking collectives: 18.2 us -> 0 us
  between operations: 13.9 us -> 0.64 us
    pallas_call x0 -> x1, Pallas kernels: none -> 279 us  [body(): pl.pallas_call(functools.partial(kernel, nz, ny, slots, pipes), out_shape...]
    all_gather x2 -> x0, waiting for transfers between devices: 154 us -> none  [the longest x1 77.8 us: body(): input_all = lax.all_gather(inputs, 'expert')]
    reduce_scatter x1 -> x0, waiting for transfers between devices: 118 us -> none  [body(): total = lax.psum_scatter(part, 'expert', scatter_dimension=0, tiled=False)]
    dot_general x8 -> x0, matrix products: 49.1 us -> none  [the longest x1 10.5 us: body(): jnp.dot(up_part, up_w.T, preferred_element_type=F32)]
    all_to_all x2 -> x0, blocking collectives: 18.2 us -> none  [the longest x1 9.1 us: body(): mine = lax.all_to_all(weights, 'expert', 0, 0, tiled=True)]
    ppermute x1 -> x0, waiting for transfers between devices: 7.39 us -> none  [body(): lax.ppermute(combined.astype(BF16), 'pipe', [(s, s - 1) for s in range(1,...]
  transfers between devices with their start and end apart: 4 -> 0, of which waited for: 4 -> 0; matrix products, arithmetic and copies ran while one was open for 3% -> 0% of each run, Pallas kernels for 0% -> 0%
where the time goes in v2:
time: 285 us
  Pallas kernels  279 us (98%)
  local copies, waits for them, and re-layouts  4.82 us (2%)
    pallas_call x1, Pallas kernels, body(): pl.pallas_call(functools.partial(kernel, nz, ny, slots, pipes), out_shape...  279 us

profile of v2, /device:TPU:24, one launch (start us, length us, event | category | flops | bytes accessed | tf_op | source)
XLA Modules:
  0.0 284.9 jit_solution(11997419793469884089)
XLA Ops:
  0.6 0.7 copy.14
  1.3 0.7 copy.13
  2.0 0.6 broadcast_in_dim.41.send_w_ref
  2.7 278.8 %shard_map.86 = (bf16[128,2560]{1,0:T(8,128)(2,1)}, f32[16,8,128]{2,1,0:T(8,128)}, bf16[16,2,128,2560]{3,2,1,0:T(8,128)(2,1)}) custom-call(bf16[128,2560]{1,0:T(8,128)(2,1)} %bitcast.31, bf16[128,2560]{1,0:T(8,128)(2,1)} %bitcast.32, f32[16,8,128]{2,1,0:T(8,128)} %broadcast_in_dim.41.send_w_ref, bf16[2560,768]{1,0:T(8,128)(2,1)} %bitcast.28, ...), custom_call_target="tpu_custom_call" | custom-call | flops 17616076800 | bytes 83886080 | tf_op jit(solution)/shard_map/pallas_call | solution.py:389
  281.5 0.8 slice.3
  282.3 0.6 select_reduce_fusion
  282.9 2.0 copy.16
  (1 shorter events, 0.0 us)

commit v3 on v2

--- a/solution.py
+++ b/solution.py
@@ -21,8 +21,8 @@
     grad_ref, input_ref, send_w_ref, gate_hbm, up_hbm, down_hbm,
     out_ref, gates_ref, all_ref,
     gate_w, up_w, down_w, blocks, rows, parts, hidden, scaled, slot_w, route, gate_send,
-    core_recv, y_send, y_recv, z_send, z_recv, total, final, zeros,
-    load_sem, own_sem, block_sem, zero_sem, ag_send, ag_recv, w_send, w_recv, g_send, g_recv,
+    core_recv, y_send, y_recv, z_send, z_recv, grad_recv,
+    load_sem, own_sem, block_sem, ag_send, ag_recv, w_send, w_recv, g_send, g_recv,
     c_send_sem, c_recv_sem, y_send_sem, y_recv_sem, z_send_sem, z_recv_sem, p_sem,
 ):
     peers = nz * ny * 2
@@ -62,7 +62,7 @@
     def y_peer(i):
         return lax.rem(yy + i, ny)
 
-    def plane_sends(z, act):
+    def line_sends(z, act):
         block = number(z, yy, core)
 
         @pl.when((z <= zz) & (zz + 1 < nz))
@@ -73,9 +73,11 @@
         def _():
             act(spread(block, 2, me - 2 * ny))
 
+    def side_sends(z, act):
+        block = number(z, yy, core)
+        act(spread(block, 0, sibling))
         for i in range(1, ny):
             act(spread(block, 2 + i, number(zz, y_peer(i), core)))
-        act(spread(block, 0, sibling))
 
     loads = [
         pltpu.make_async_copy(gate_hbm, gate_w, load_sem.at[0]),
@@ -95,16 +97,17 @@
     def _(i):
         pl.semaphore_signal(barrier, inc=1, device_id={"expert": lax.rem(me + i, peers)}, device_id_type=MESH)
 
-    @pl.when(stage > 0)
-    def _():
-        pl.semaphore_signal(barrier, inc=1, device_id={"pipe": stage - 1}, device_id_type=MESH)
-
-    @pl.when(stage < pipes - 1)
-    def _():
-        pl.semaphore_signal(barrier, inc=1, device_id={"pipe": stage + 1}, device_id_type=MESH)
-
-    beside = jnp.where(stage > 0, 1, 0) + jnp.where(stage < pipes - 1, 1, 0)
-    pl.semaphore_wait(barrier, peers - 1 + beside)
+    earlier = lax.rem(stage + pipes - 1, pipes)
+    later = lax.rem(stage + 1, pipes)
+
+    @pl.loop(0, nz)
+    def _(z):
+        for other in (earlier, later):
+            pl.semaphore_signal(
+                barrier, inc=1, device_id={"pipe": other, "expert": number(z, yy, core)}, device_id_type=MESH
+            )
+
+    pl.semaphore_wait(barrier, peers - 1 + 2 * nz)
 
     def w_copy(target):
         return remote(send_w_ref.at[target], route.at[me], w_send.at[target], w_recv.at[me], target)
@@ -118,7 +121,13 @@
 
     for copy in own:
         copy.wait()
-    plane_sends(zz, lambda c: c.start())
+    line_sends(zz, lambda c: c.start())
+    side_sends(zz, lambda c: c.start())
+    passing = pltpu.make_async_remote_copy(
+        src_ref=grad_ref, dst_ref=grad_recv, send_sem=p_sem.at[0], recv_sem=p_sem.at[1],
+        device_id={"pipe": earlier}, device_id_type=MESH,
+    )
+    passing.start()
     route[me] = send_w_ref[me]
 
     @pl.loop(1, peers)
@@ -139,21 +148,25 @@
         place = dot(used.astype(BF16), before)[0:1].astype(jnp.int32)
         return (place == slot_at) & (weight[0:1] > 0), weight[0:1]
 
-    def block_in(z, i):
-        return number(z, lax.rem(i, ny), lax.div(i, ny))
-
-    def fetch(z, i):
-        return pltpu.make_async_copy(all_ref.at[block_in(z, i)], blocks.at[i], block_sem.at[i])
-
-    def compute(z):
-        @pl.loop(0, count)
+    def block_in(g, i):
+        k = lax.div(i, 2)
+        z = jnp.where(k == 0, column_of(g), column_of(jnp.maximum(g - 1, 0)))
+        return number(z, lax.rem(yy + k, ny), lax.rem(i, 2))
+
+    def fetch(g, i):
+        return pltpu.make_async_copy(all_ref.at[block_in(g, i)], blocks.at[i], block_sem.at[i])
+
+    def compute(g, first, last):
+        span = pl.ds(first * slots, (last - first) * slots)
+
+        @pl.loop(first, last)
         def _(i):
-            fetch(z, i).start()
-
-        @pl.loop(0, count)
+            fetch(g, i).start()
+
+        @pl.loop(first, last)
         def _(i):
-            fetch(z, i).wait()
-            pick, weight = pick_of(block_in(z, i))
+            fetch(g, i).wait()
+            pick, weight = pick_of(block_in(g, i))
             pick16 = jnp.where(pick, 1.0, 0.0).astype(BF16)
             at = pl.ds(pl.multiple_of(i * slots, slots), slots)
             rows[0, at] = dot(pick16, blocks[i, 0]).astype(BF16)
@@ -167,32 +180,32 @@
         @pl.loop(0, inner // tile)
         def _(f):
             at = pl.ds(pl.multiple_of(f * tile, tile), tile)
-            gate_pre = dot(rows[1], gate_w[:, at])
-            up_pre = dot(rows[1], up_w[:, at])
-            back = dot(rows[0], down_w[at, :], NT)
+            gate_pre = dot(rows[1, span], gate_w[:, at])
+            up_pre = dot(rows[1, span], up_w[:, at])
+            back = dot(rows[0, span], down_w[at, :], NT)
             sig = jax.nn.sigmoid(gate_pre)
             up_back = back * (gate_pre * sig)
-            hidden[0, :, at] = (back * up_pre * sig * (1.0 + gate_pre * (1.0 - sig))).astype(BF16)
-            hidden[1, :, at] = up_back.astype(BF16)
+            hidden[0, span, at] = (back * up_pre * sig * (1.0 + gate_pre * (1.0 - sig))).astype(BF16)
+            hidden[1, span, at] = up_back.astype(BF16)
             value = jnp.sum(up_back * up_pre, axis=1, keepdims=True)
-            slot_w[1] = slot_w[1] + jnp.broadcast_to(value, slot_w[1].shape)
+            slot_w[1, span] = slot_w[1, span] + jnp.broadcast_to(value, (value.shape[0], 128))
 
         wide = 512
 
         @pl.loop(0, width // wide)
         def _(d):
             at = pl.ds(pl.multiple_of(d * wide, wide), wide)
-            back = dot(hidden[0], gate_w[at, :], NT) + dot(hidden[1], up_w[at, :], NT)
-            back = back.astype(BF16).astype(F32) * slot_w[0, :, 0:1]
-            scaled[:, at] = back.astype(BF16)
-
-        @pl.loop(0, count)
+            back = dot(hidden[0, span], gate_w[at, :], NT) + dot(hidden[1, span], up_w[at, :], NT)
+            back = back.astype(BF16).astype(F32) * slot_w[0, span, 0:1]
+            scaled[span, at] = back.astype(BF16)
+
+        @pl.loop(first, last)
         def _(i):
-            block = block_in(z, i)
+            block = block_in(g, i)
             pick, weight = pick_of(block)
             turned = jnp.where(pick, 1.0, 0.0).T.astype(BF16)
             at = pl.ds(pl.multiple_of(i * slots, slots), slots)
-            parts[lax.div(i, ny), lax.rem(i, ny)] = dot(turned, scaled[at]).astype(BF16)
+            parts[lax.rem(i, 2), lax.div(i, 2)] = dot(turned, scaled[at]).astype(BF16)
             value = jnp.sum(jnp.where(pick, slot_w[1, at, 0:1], 0.0), axis=0, keepdims=True)
             gate_send[block] = jnp.broadcast_to(value, (8, tokens))
 
@@ -203,92 +216,108 @@
         def _(r):
             act(pl.ds(pl.multiple_of(r * step, step), step))
 
-    def core_copy(j):
-        slot = lax.rem(j, 2)
-        return remote(parts.at[1 - core], core_recv.at[slot], c_send_sem.at[slot], c_recv_sem.at[slot], sibling)
+    def core_copy(g, first, last):
+        slot = lax.rem(g, 2)
+        entries = pl.ds(first // 2, (last - first) // 2)
+        return remote(
+            parts.at[1 - core, entries], core_recv.at[slot, entries],
+            c_send_sem.at[slot], c_recv_sem.at[slot], sibling,
+        )
 
     def y_copy(j, i):
         return remote(
-            y_send.at[j, y_peer(i)], y_recv.at[j, ny - 1 - i],
+            y_send.at[j, i], y_recv.at[j, ny - 1 - i],
             y_send_sem.at[j, i - 1], y_recv_sem.at[j, ny - 1 - i], number(zz, y_peer(i), core),
         )
 
-    def core_finish(j):
-        core_copy(j).wait()
-        slot = lax.rem(j, 2)
-        for y in range(ny):
-
+    def core_finish(g, first, last):
+        core_copy(g, first, last).wait()
+        slot = lax.rem(g, 2)
+
+        def entry(k, j):
             def act(at):
-                both = parts[core, y, at].astype(F32) + core_recv[slot, y, at].astype(F32)
-                y_send[j, y, at] = both.astype(BF16)
+                both = parts[core, k, at].astype(F32) + core_recv[slot, k, at].astype(F32)
+                y_send[j, k, at] = both.astype(BF16)
 
             by_rows(act)
-        for i in range(1, ny):
-            y_copy(j, i).start()
+
+        for k in range(max(1, first // 2), last // 2):
+            entry(k, g - 1)
+            y_copy(g - 1, k).start()
+        if first == 0:
+            entry(0, g)
 
     def z_copy(z):
-        return remote(
-            z_send.at[z], z_recv.at[zz], z_send_sem.at[z], z_recv_sem.at[zz], number(z, yy, core)
+        return pltpu.make_async_remote_copy(
+            src_ref=z_send.at[z], dst_ref=z_recv.at[zz], send_sem=z_send_sem.at[z], recv_sem=z_recv_sem.at[zz],
+            device_id={"pipe": earlier, "expert": number(z, yy, core)}, device_id_type=MESH,
         )
 
     def z_from(z):
-        return remote(z_send.at[z], z_recv.at[z], z_send_sem.at[z], z_recv_sem.at[z], number(z, yy, core))
+        return pltpu.make_async_remote_copy(
+            src_ref=z_send.at[z], dst_ref=z_recv.at[z], send_sem=z_send_sem.at[z], recv_sem=z_recv_sem.at[z],
+            device_id={"pipe": earlier, "expert": number(z, yy, core)}, device_id_type=MESH,
+        )
 
     def y_finish(j):
         z = column_of(j)
         for i in range(1, ny):
             y_copy(j, i).wait_recv()
 
-        def summed(at):
-            value = y_send[j, yy, at].astype(F32)
+        def act(at):
+            value = y_send[j, 0, at].astype(F32)
             for i in range(ny - 1):
                 value = value + y_recv[j, i, at].astype(F32)
-            return value
-
-        @pl.when(z == zz)
-        def _():
-            def act(at):
-                total[at] = summed(at)
-
-            by_rows(act)
-
-        @pl.when(z != zz)
-        def _():
-            def act(at):
-                z_send[z, at] = summed(at).astype(BF16)
-
-            by_rows(act)
-            z_copy(z).start()
-
-    @pl.loop(0, nz)
-    def _(j):
-        far = j + 1
-
-        @pl.when(zz - far >= 0)
-        def _():
-            arrived(number(zz - far, yy, core))
-            plane_sends(zz - far, lambda c: c.start())
-
-        @pl.when(zz + far < nz)
-        def _():
-            arrived(number(zz + far, yy, core))
-            plane_sends(zz + far, lambda c: c.start())
-
-        z = column_of(j)
+            z_send[z, at] = value.astype(BF16)
+
+        by_rows(act)
+        z_copy(z).start()
+
+    arrived(number(zz, yy, 1 - core))
+    compute(0, 0, 2)
+    core_copy(0, 0, 2).start()
+    core_finish(0, 0, 2)
+
+    def others_in(z):
         for i in range(1, ny):
             block = number(z, y_peer(i), core)
             arrived(block)
             spread(block, 0, sibling).start()
-        for y in range(ny):
-            arrived(number(z, y, 1 - core))
-        compute(z)
-        core_copy(j).start()
-
-        @pl.when(j > 0)
+
+    @pl.loop(1, nz)
+    def _(g):
+        @pl.when(zz - g >= 0)
         def _():
-            y_finish(j - 1)
-
-        core_finish(j)
+            arrived(number(zz - g, yy, core))
+            line_sends(zz - g, lambda c: c.start())
+
+        @pl.when(zz + g < nz)
+        def _():
+            arrived(number(zz + g, yy, core))
+            line_sends(zz + g, lambda c: c.start())
+
+        z = column_of(g)
+        side_sends(z, lambda c: c.start())
+        others_in(column_of(g - 1))
+        arrived(number(z, yy, 1 - core))
+        for i in range(1, ny):
+            arrived(number(column_of(g - 1), y_peer(i), 1 - core))
+        compute(g, 0, count)
+        core_copy(g, 0, count).start()
+
+        @pl.when(g > 1)
+        def _():
+            y_finish(g - 2)
+
+        core_finish(g, 0, count)
+
+    others_in(column_of(nz - 1))
+    for i in range(1, ny):
+        arrived(number(column_of(nz - 1), y_peer(i), 1 - core))
+    compute(nz, 2, count)
+    core_copy(nz, 2, count).start()
+    core_finish(nz, 2, count)
+    y_finish(nz - 2)
 
     def g_copy(target):
         return remote(gate_send.at[target], gates_ref.at[me], g_send.at[target], g_recv.at[me], target)
@@ -301,41 +330,26 @@
         g_copy(lax.rem(me + i, peers)).start()
 
     gates_ref[me] = gate_send[me]
-    own_grad = pltpu.make_async_copy(grad_ref, blocks.at[0, 0], own_sem.at[0])
-    own_grad.start()
+    y_finish(nz - 1)
+    passing.wait_recv()
+
+    @pl.loop(0, nz)
+    def _(z):
+        z_from(z).wait_recv()
 
     @pl.when(stage == pipes - 1)
     def _():
-        zeros[...] = jnp.zeros_like(zeros)
-        pltpu.make_async_copy(zeros, out_ref, zero_sem).start()
-
-    y_finish(nz - 1)
-    own_grad.wait()
-
-    @pl.loop(0, nz)
-    def _(z):
-        @pl.when(z != zz)
-        def _():
-            z_from(z).wait_recv()
-
-    z_recv[zz] = jnp.zeros_like(z_recv[0])
-
-    def finish(at):
-        value = blocks[0, 0, at].astype(F32) + total[at]
-        for z in range(nz):
-            value = value + z_recv[z, at].astype(F32)
-        final[at] = value.astype(BF16)
-
-    by_rows(finish)
-
-    passing = pltpu.make_async_remote_copy(
-        src_ref=final, dst_ref=out_ref, send_sem=p_sem.at[0], recv_sem=p_sem.at[1],
-        device_id={"pipe": lax.rem(stage + pipes - 1, pipes)}, device_id_type=MESH,
-    )
-
-    @pl.when(stage > 0)
+        out_ref[...] = jnp.zeros_like(out_ref)
+
+    @pl.when(stage < pipes - 1)
     def _():
-        passing.start()
+        def finish(at):
+            value = grad_recv[at].astype(F32)
+            for z in range(nz):
+                value = value + z_recv[z, at].astype(F32)
+            out_ref[at] = value.astype(BF16)
+
+        by_rows(finish)
 
     @pl.loop(1, peers)
     def _(i):
@@ -346,26 +360,14 @@
 
     @pl.loop(0, nz)
     def _(z):
-        plane_sends(z, lambda c: c.wait_send())
+        line_sends(z, lambda c: c.wait_send())
+        side_sends(z, lambda c: c.wait_send())
         for i in range(1, ny):
             spread(number(z, y_peer(i), core), 0, sibling).wait_send()
             y_copy(z, i).wait_send()
-
-        @pl.when(z != zz)
-        def _():
-            z_copy(z).wait_send()
-
-    @pl.when(stage > 0)
-    def _():
-        passing.wait_send()
-
-    @pl.when(stage < pipes - 1)
-    def _():
-        passing.wait_recv()
-
-    @pl.when(stage == pipes - 1)
-    def _():
-        pltpu.make_async_copy(zeros, out_ref, zero_sem).wait()
+        z_copy(z).wait_send()
+
+    passing.wait_send()
 
 
 def body(pipes, out_grad, layer_input, route_ids, route_probs, gate_weight, up_weight, down_weight):
@@ -394,7 +396,7 @@
             jax.ShapeDtypeStruct((peers, 2) + half, BF16),
         ),
         in_specs=[anywhere, anywhere, vmem, anywhere, anywhere, anywhere],
-        out_specs=(anywhere, vmem, anywhere),
+        out_specs=(vmem, vmem, anywhere),
         scratch_shapes=[
             pltpu.VMEM((width, inner), BF16),
             pltpu.VMEM((width, inner), BF16),
@@ -412,10 +414,8 @@
             pltpu.VMEM((nz, ny - 1) + half, BF16),
             pltpu.VMEM((nz,) + half, BF16),
             pltpu.VMEM((nz,) + half, BF16),
-            pltpu.VMEM(half, F32),
             pltpu.VMEM(half, BF16),
-            pltpu.VMEM(half, BF16),
-            dma((3,)), dma((2,)), dma((count,)), dma(()),
+            dma((3,)), dma((2,)), dma((count,)),
             dma((peers, 2 + ny)), dma((peers,)), dma((peers,)), dma((peers,)),
             dma((peers,)), dma((peers,)),
             dma((2,)), dma((2,)), dma((nz, ny - 1)), dma((nz, ny - 1)), dma((nz,)), dma((nz,)), dma((2,)),

time: 285 us -> 273 us (0.958)
  Pallas kernels: 279 us -> 266 us
    pallas_call x1, Pallas kernels: 279 us -> 266 us  [body(): pl.pallas_call(functools.partial(kernel, nz, ny, slots, pipes), out_shape...]
where the time goes in v3:
time: 273 us; the launch traced here: 272 us
  Pallas kernels  266 us (97%)
  local copies, waits for them, and re-layouts  4.82 us (2%)
    pallas_call x1, Pallas kernels, body(): pl.pallas_call(functools.partial(kernel, nz, ny, slots, pipes), out_shape...  266 us

profile of v3, /device:TPU:24, one launch (start us, length us, event | category | flops | bytes accessed | tf_op | source)
XLA Modules:
  0.0 272.0 jit_solution(14858291346261810068)
XLA Ops:
  0.6 0.7 copy.14
  1.3 0.7 copy.13
  2.0 0.6 broadcast_in_dim.41.send_w_ref
  2.7 265.9 %shard_map.86 = (bf16[128,2560]{1,0:T(8,128)(2,1)}, f32[16,8,128]{2,1,0:T(8,128)}, bf16[16,2,128,2560]{3,2,1,0:T(8,128)(2,1)}) custom-call(bf16[128,2560]{1,0:T(8,128)(2,1)} %bitcast.31, bf16[128,2560]{1,0:T(8,128)(2,1)} %bitcast.32, f32[16,8,128]{2,1,0:T(8,128)} %broadcast_in_dim.41.send_w_ref, bf16[2560,768]{1,0:T(8,128)(2,1)} %bitcast.28, ...), custom_call_target="tpu_custom_call" | custom-call | flops 17616076800 | bytes 83886080 | tf_op jit(solution)/shard_map/pallas_call | solution.py:391
  268.6 0.8 slice.3
  269.4 0.6 select_reduce_fusion
  270.0 2.0 copy.16
  (1 shorter events, 0.0 us)

commit v4 on v3

--- a/solution.py
+++ b/solution.py
@@ -156,7 +156,7 @@
     def fetch(g, i):
         return pltpu.make_async_copy(all_ref.at[block_in(g, i)], blocks.at[i], block_sem.at[i])
 
-    def compute(g, first, last):
+    def compute(g, first, last, between=lambda: None):
         span = pl.ds(first * slots, (last - first) * slots)
 
         @pl.loop(first, last)
@@ -190,6 +190,7 @@
             value = jnp.sum(up_back * up_pre, axis=1, keepdims=True)
             slot_w[1, span] = slot_w[1, span] + jnp.broadcast_to(value, (value.shape[0], 128))
 
+        between()
         wide = 512
 
         @pl.loop(0, width // wide)
@@ -284,8 +285,7 @@
             arrived(block)
             spread(block, 0, sibling).start()
 
-    @pl.loop(1, nz)
-    def _(g):
+    def advance(g):
         @pl.when(zz - g >= 0)
         def _():
             arrived(number(zz - g, yy, core))
@@ -296,13 +296,23 @@
             arrived(number(zz + g, yy, core))
             line_sends(zz + g, lambda c: c.start())
 
+        side_sends(column_of(g), lambda c: c.start())
+
+    advance(1)
+
+    @pl.loop(1, nz)
+    def _(g):
+        def between():
+            @pl.when(g + 1 < nz)
+            def _():
+                advance(g + 1)
+
         z = column_of(g)
-        side_sends(z, lambda c: c.start())
         others_in(column_of(g - 1))
         arrived(number(z, yy, 1 - core))
         for i in range(1, ny):
             arrived(number(column_of(g - 1), y_peer(i), 1 - core))
-        compute(g, 0, count)
+        compute(g, 0, count, between)
         core_copy(g, 0, count).start()
 
         @pl.when(g > 1)

time: 273 us -> 273 us (level)
  no operation moved by 1% of the time
where the time goes in v4:
time: 273 us
  Pallas kernels  267 us (98%)
  local copies, waits for them, and re-layouts  4.82 us (2%)
    pallas_call x1, Pallas kernels, body(): pl.pallas_call(functools.partial(kernel, nz, ny, slots, pipes), out_shape...  267 us

profile of v4, /device:TPU:24, one launch (start us, length us, event | category | flops | bytes accessed | tf_op | source)
XLA Modules:
  0.0 272.7 jit_solution(5885976737160269612)
XLA Ops:
  0.6 0.7 copy.14
  1.3 0.7 copy.13
  2.0 0.6 broadcast_in_dim.41.send_w_ref
  2.7 266.6 %shard_map.86 = (bf16[128,2560]{1,0:T(8,128)(2,1)}, f32[16,8,128]{2,1,0:T(8,128)}, bf16[16,2,128,2560]{3,2,1,0:T(8,128)(2,1)}) custom-call(bf16[128,2560]{1,0:T(8,128)(2,1)} %bitcast.31, bf16[128,2560]{1,0:T(8,128)(2,1)} %bitcast.32, f32[16,8,128]{2,1,0:T(8,128)} %broadcast_in_dim.41.send_w_ref, bf16[2560,768]{1,0:T(8,128)(2,1)} %bitcast.28, ...), custom_call_target="tpu_custom_call" | custom-call | flops 17616076800 | bytes 83886080 | tf_op jit(solution)/shard_map/pallas_call | solution.py:401
  269.3 0.8 slice.3
  270.1 0.6 select_reduce_fusion
  270.8 2.0 copy.16
  (1 shorter events, 0.0 us)
